TPU v7x, 32 devices: a whole 2x2x4 slice. The times are simulated.
32 devices in a mesh: pole: 2 (over x), prow: 4 (over y, core), pcol: 4 (over z).
Axes of the slice: x: 2, y: 2, z: 4, core: 2. Of those that a mesh axis runs over, the one named last changes fastest.
Arguments:
- root_inverse: float32 [6144, 3072], P(('pole', 'prow'), 'pcol'), parts along dimension 0, may hold values from -6 to 6, as said below
- lower_blocks: float32 [6144, 1024], P(('pole', 'pcol'), 'prow'), parts along dimension 0, may hold values from -0.109375 to 0.109375
- block_pattern: int32 [12, 4], replicated, may hold values 0 or 1
- diag_inverse: float32 [8, 256, 256], P(('pole', 'pcol'), 'prow'), parts along dimension 0, may hold values from -6 to 6, as said below
Outputs:
- selected: float32 [6144, 1024], P(('pole', 'prow'), 'pcol'), parts along dimension 0
- diagonal_blocks: float32 [8, 256, 256], P(('pole', 'pcol'), 'prow'), parts along dimension 0
There are 2 independent parts, one for each index of `pole`. A program takes and returns all parts, laid end to end along the dimension named above; an argument that names none is the same for every part. Nothing has to cross between parts.
Inputs may be any that keep to these rules, and one draw needn't show every extreme that they name: `root_inverse`: symmetric. `diag_inverse`: each block symmetric.
All inputs are finite; a program needn't handle non-finite values.
Results may differ from a plain program's by a relative error of at most 0.000071.
Values sent between devices are 32-bit elements; how exact they have to be, the bound alone decides.
A program may use at most 128 MiB of HBM per device.

v0:
```python
import jax
import jax.numpy as jnp
from jax import lax
from jax.sharding import PartitionSpec as P

B = 256


def broadcast(value, axis, source):
    kept = jnp.where(lax.axis_index(axis) == source, value, 0).astype(value.dtype)
    return lax.psum(kept, axis)


def supernode_terms(lower_rows, upper_rows, width):
    lower_split = lower_rows.reshape(lower_rows.shape[0], -1, width)
    upper_split = upper_rows.reshape(upper_rows.shape[0], -1, width)
    return jnp.einsum("isa,isb->sab", lower_split, upper_split, precision=lax.Precision.HIGHEST)


def on_device(root_inverse, lower_blocks, block_pattern, diag_inverse):
    row_count = lax.axis_size("prow")
    column_count = lax.axis_size("pcol")
    row_index = lax.axis_index("prow")
    column_index = lax.axis_index("pcol")
    local_rows = lower_blocks.shape[0]
    local_columns = lower_blocks.shape[1]
    panel_rows = root_inverse.shape[0]
    total_columns = local_columns * row_count
    owned_columns = total_columns // column_count
    block_total = block_pattern.shape[0]
    supernode_total = block_pattern.shape[1]
    row_blocks = (column_index * local_rows + jnp.arange(local_rows, dtype=jnp.int32)) // B
    column_blocks = (row_index * local_columns + jnp.arange(local_columns, dtype=jnp.int32)) // B
    row_select = (row_blocks[:, None] == jnp.arange(block_total, dtype=jnp.int32)[None, :]).astype(
        jnp.float32
    )
    column_select = (
        jnp.arange(supernode_total, dtype=jnp.int32)[:, None] == column_blocks[None, :]
    ).astype(jnp.float32)
    block_mask = jnp.dot(
        jnp.dot(row_select, block_pattern.astype(jnp.float32), precision=lax.Precision.HIGHEST),
        column_select,
        precision=lax.Precision.HIGHEST,
    )
    masked = lower_blocks * block_mask
    gathered = lax.all_gather(masked, "prow", axis=1, tiled=True)
    row_ratio = row_count // column_count
    source = row_index // row_ratio
    cross_rows = lax.dynamic_slice_in_dim(
        gathered, row_index % row_ratio * panel_rows, panel_rows, 0
    )
    shares = lax.psum_scatter(
        lax.dot_general(
            gathered,
            root_inverse,
            (((0,), (1,)), ((), ())),
            precision=lax.Precision.HIGHEST,
            preferred_element_type=jnp.float32,
        ),
        "pcol",
        scatter_dimension=0,
        tiled=True,
    )
    selected = -shares.T
    wanted = broadcast(cross_rows, "pcol", source)
    own_rows = lax.dynamic_slice_in_dim(wanted, column_index * owned_columns, owned_columns, 1)
    product = supernode_terms(own_rows, selected, B)
    correction = lax.psum_scatter(product, "prow", scatter_dimension=1, tiled=True)
    return (selected, diag_inverse - correction)


def solution(mesh):
    placed = (
        P(("pole", "prow"), "pcol"),
        P(("pole", "pcol"), "prow"),
        P(),
        P(("pole", "pcol"), "prow", None),
    )
    return jax.shard_map(
        on_device,
        mesh=mesh,
        in_specs=placed,
        out_specs=(P(("pole", "prow"), "pcol"), P(("pole", "pcol"), "prow", None)),
        check_vma=False,
    )
```

profile of v0, /device:TPU:29, one launch (start us, length us, event | category | flops | bytes accessed | tf_op | source)
XLA Modules:
  0.0 258.2 jit_solution(12395347870411656472)
XLA Ops:
  7.2 0.0 copy-start
  7.2 0.0 all-gather.2.cloned.1.call-start
  7.3 1.2 fusion.2
  8.5 2.5 convolution_multiply_fusion
  11.0 0.0 all-gather.2.cloned.1.call-update
  11.0 0.0 all-reduce.2.cloned.1.call-start
  11.0 29.1 %all-gather.2.cloned.1.call-done = f32[768,1024]{1,0:T(8,128)} async-done(((f32[768,256]{1,0:T(8,128)}), f32[768,1024]{1,0:T(8,128)}) %all-gather.2.cloned.1.call-update) | async-done | bytes 3145744 | tf_op jit(solution)/shard_map/all_gather | solution.py:46
  40.1 4.1 %broadcast_select_fusion = f32[768,1024]{1,0:T(8,128)} fusion(f32[768,1024]{1,0:T(8,128)} %all-gather.2.cloned.1.call-done, pred[]{:T(512)S(6)} %eq.37), kind=kLoop, calls=%fused_computation | loop fusion | flops 786432 | bytes 6291457 | tf_op jit(solution)/shard_map/jit(_where)/select_n | solution.py:10
  44.2 0.0 all-reduce.2.cloned.1.call-update
  44.2 0.0 reduce-scatter.3.cloned.1.call-start
  44.3 0.0 copy-done
  44.3 17.5 %fusion.10 = f32[1024,768]{1,0:T(8,128)} fusion(f32[768,1024]{1,0:T(8,128)} %all-gather.2.cloned.1.call-done, f32[768,768]{1,0:T(8,128)S(1)} %copy-done), kind=kOutput, calls=%fused_computation.26 | convolution fusion | flops 7247757312 | bytes 8650752 | tf_op jit(solution)/shard_map/dot_general | solution.py:53
  61.8 0.0 reduce-scatter.3.cloned.1.call-update
  61.9 0.0 copy-start.1
  61.9 0.0 reduce-scatter.5.cloned.1.call-start
  61.9 102.1 %all-reduce.2.cloned.1.call-done = f32[768,1024]{1,0:T(8,128)} async-done(((f32[768,1024]{1,0:T(8,128)}), f32[768,1024]{1,0:T(8,128)}) %all-reduce.2.cloned.1.call-update) | async-done | bytes 3145744 | tf_op jit(solution)/shard_map/psum | solution.py:11
  164.1 62.5 %reduce-scatter.3.cloned.1.call-done = f32[256,768]{1,0:T(8,128)} async-done(((f32[1024,768]{1,0:T(8,128)}), f32[256,768]{1,0:T(8,128)}) %reduce-scatter.3.cloned.1.call-update) | async-done | bytes 786448 | tf_op jit(solution)/shard_map/reduce_scatter | solution.py:52
  226.5 3.5 %convolution_bitcast_fusion = f32[1,256,256]{2,1,0:T(8,128)} fusion(f32[768,1024]{1,0:T(8,128)} %all-reduce.2.cloned.1.call-done, s32[]{:T(128)S(6)} %select_n.41, f32[256,768]{1,0:T(8,128)} %reduce-scatter.3.cloned.1.call-done), kind=kOutput, calls=%fused_computation.2 | convolution fusion | flops 604176384 | bytes 1835012 | tf_op jit(solution)/shard_map/isa,isb->sab/dot_general | solution.py:17
  230.0 0.0 reduce-scatter.5.cloned.1.call-update
  230.0 1.2 negate_bitcast_fusion
  231.2 1.1 copy.6
  232.4 17.9 %reduce-scatter.5.cloned.1.call-done = f32[1,64,256]{2,1,0:T(8,128)} async-done(((f32[1,256,256]{2,1,0:T(8,128)}), f32[1,64,256]{2,1,0:T(8,128)}) %reduce-scatter.5.cloned.1.call-update) | async-done | bytes 65552 | tf_op jit(solution)/shard_map/reduce_scatter | solution.py:68
  250.2 0.0 copy-done.1
  250.2 1.5 sub.19
  (2 shorter events, 0.0 us)
Async XLA Ops:
  7.2 37.1 %copy-start = (f32[768,768]{1,0:T(8,128)S(1)}, f32[768,768]{1,0:T(8,128)}, u32[]{:S(2)}) copy-start(f32[768,768]{1,0:T(8,128)} %param.4) | copy-start | bytes 7077892
  7.2 32.9 %all-gather.2.cloned.1.call-start = ((), (), s32[]{:S(2)}) async-start(), calls=%async_computation.2 | async-start | bytes 3932160 | tf_op jit(solution)/shard_map/all_gather | solution.py:46
  11.0 153.1 %all-reduce.2.cloned.1.call-start = ((), (), s32[]{:S(2)}) async-start(), calls=%async_computation.4 | async-start | bytes 6291456 | tf_op jit(solution)/shard_map/psum | solution.py:11
  44.2 182.3 %reduce-scatter.3.cloned.1.call-start = ((), (), s32[]{:S(2)}) async-start(), calls=%async_computation.3 | async-start | bytes 3932160 | tf_op jit(solution)/shard_map/reduce_scatter | solution.py:52
  61.9 188.4 %copy-start.1 = (f32[1,64,256]{2,1,0:T(8,128)S(1)}, f32[1,64,256]{2,1,0:T(8,128)}, u32[]{:S(2)}) copy-start(f32[1,64,256]{2,1,0:T(8,128)} %param.7) | copy-start | bytes 196612
  61.9 188.3 %reduce-scatter.5.cloned.1.call-start = ((), (), s32[]{:S(2)}) async-start(), calls=%async_computation.5 | async-start | bytes 327680 | tf_op jit(solution)/shard_map/reduce_scatter | solution.py:68
Sparse Core Ops, SparseCore 0:
  11.1 28.9 all-gather.1
  44.4 119.6 all-reduce.1
  166.4 60.1 reduce-scatter.2
  230.2 20.0 reduce-scatter.4
where the time goes:
time: 261 us; the launch traced here: 258 us
  waiting for transfers between devices  212 us (81%)
  matrix products  24.7 us (9%)
  between operations  13.8 us (5%)
  other arithmetic  6.8 us (3%)
    psum x1, waiting for transfers between devices, broadcast(): return lax.psum(kept, axis)  102 us
    reduce_scatter x1, waiting for transfers between devices, on_device(): lax.psum_scatter(lax.dot_general(gathered, root_inverse, (((0,), (1,)), (...  62.5 us
    all_gather x1, waiting for transfers between devices, on_device(): gathered = lax.all_gather(masked, 'prow', axis=1, tiled=True)  29.1 us
    reduce_scatter x1, waiting for transfers between devices, on_device(): lax.psum_scatter(product, 'prow', scatter_dimension=1, tiled=True)  17.9 us
    dot_general x1, matrix products, on_device(): lax.dot_general(gathered, root_inverse, (((0,), (1,)), ((), ())), precisi...  17.5 us
  transfers between devices with their start and end apart: 4, of which 4 were waited for; matrix products, arithmetic and copies ran while one was open for 8% of the time, Pallas kernels for 0%

commit v1 on v0

v1 whole, which is shorter than its diff:
```python
import functools

import jax
import jax.numpy as jnp
from jax import lax
from jax.experimental import pallas as pl
from jax.experimental.pallas import tpu as pltpu
from jax.sharding import PartitionSpec as P

B = 256
MESH = pl.DeviceIdType.MESH


def split(value):
    high = value.astype(jnp.bfloat16)
    return high, (value - high.astype(jnp.float32)).astype(jnp.bfloat16)


def dot3(ahi, alo, bhi, blo):
    dot = functools.partial(jnp.dot, preferred_element_type=jnp.float32)
    return dot(ahi, bhi) + (dot(ahi, blo) + dot(alo, bhi))


def kernel(
    PR, PC, H,
    pattern, root, lower, diag, sel, out,
    G, part, recv, rhi, rlo, lhi, llo, X, xthi, xtlo, D, E,
    ygs, ygr, fws, fwr, chs, chr_, xs, xr, ds_, dr,
):
    x = lax.axis_index("pole")
    p = lax.axis_index("prow")
    c = lax.axis_index("pcol")
    Y = PR // 2
    q = PR // PC if PR > PC else 1
    y, core = p // 2, p % 2
    mate = y * 2 + (1 - core)
    local_rows, local_cols = lower.shape
    panel = root.shape[0]
    hr = panel // H
    ratio = local_rows // panel
    pc = p // ratio
    row_off = pl.multiple_of(p % ratio * panel, panel)

    def remote(src, dst, ss, rs, pp, cc):
        return pltpu.make_async_remote_copy(
            src_ref=src, dst_ref=dst, send_sem=ss, recv_sem=rs,
            device_id=(x, pp, cc), device_id_type=MESH,
        )

    barrier = pltpu.get_barrier_semaphore()
    for t in range(1, PR):
        pl.semaphore_signal(barrier, inc=1, device_id=(x, (p + t) % PR, c), device_id_type=MESH)
    for t in range(1, PC):
        pl.semaphore_signal(barrier, inc=1, device_id=(x, p, (c + t) % PC), device_id_type=MESH)

    supernode = p * local_cols // B
    for r in range(local_rows // B):
        keep = pattern[c * (local_rows // B) + r, supernode].astype(jnp.float32)
        G[p, r * B:(r + 1) * B, :] = lower[r * B:(r + 1) * B, :] * keep
    pl.semaphore_wait(barrier, PR + PC - 2)

    def y_copy(t):
        return remote(G.at[p], G.at[p], ygs.at[t], ygr.at[t], (y + t) % Y * 2 + core, c)

    def forward(yy):
        b = yy * 2 + core
        return remote(G.at[b], G.at[b], fws.at[yy], fwr.at[yy], mate, c)

    for t in range(1, Y):
        y_copy(t).start()
    forward(y).start()

    def split_root(h, carry):
        rows = pl.ds(pl.multiple_of(h * hr, hr), hr)
        rhi[rows, :], rlo[rows, :] = split(root[rows, :])
        return carry

    lax.fori_loop(0, H, split_root, 0)

    def chain(u, h):
        j = u // q
        rows = pl.ds(pl.multiple_of(h * hr, hr), hr)
        target = jnp.where(j > c, c + 1, c - 1)
        slot = jnp.where((j < c) & (j == c - 1), PR + u % q, u)
        return remote(
            part.at[u, rows], recv.at[slot, rows], chs.at[u, h], chr_.at[slot, h], p, target
        )

    def arrive(slot, h):
        rows = pl.ds(pl.multiple_of(h * hr, hr), hr)
        remote(
            recv.at[slot, rows], recv.at[slot, rows], chs.at[0, h], chr_.at[slot, h], p, c
        ).wait_recv()

    def x_copy(u):
        return remote(
            G.at[u, pl.ds(row_off, panel)], X.at[u % q], xs.at[u], xr.at[u % q], p, u // q
        )

    def phase(t, carry):
        yy = (y + Y - t) % Y

        @pl.when(t > 0)
        def _():
            remote(G.at[p], G.at[yy * 2 + core], ygs.at[t], ygr.at[t], p, c).wait_recv()
            forward(yy).start()

        other = yy * 2 + (1 - core)
        remote(G.at[other], G.at[other], fws.at[yy], fwr.at[yy], p, c).wait_recv()
        for i in range(2):
            u = yy * 2 + i

            @pl.when((c == pc) & (u // q != c))
            def _():
                x_copy(u).start()

            lhi[i], llo[i] = split(G[u])

        def chunk(h, inner):
            rows = pl.ds(pl.multiple_of(h * hr, hr), hr)
            for i in range(2):
                u = yy * 2 + i
                j = u // q
                part[u, rows, :] = dot3(rhi[rows, :], rlo[rows, :], lhi[i], llo[i])

                @pl.when(((j > c) & (c > 0)) | ((j < c) & (c < PC - 1)))
                def _():
                    arrive(u, h)
                    part[u, rows, :] += recv[u, rows, :]

                @pl.when(j != c)
                def _():
                    chain(u, h).start()

            return inner

        lax.fori_loop(0, H, chunk, 0)
        return carry

    lax.fori_loop(0, Y, phase, 0)

    for i in range(q):
        @pl.when(c == pc)
        def _():
            X[i] = G[c * q + i, pl.ds(row_off, panel), :]

        @pl.when(c != pc)
        def _():
            remote(X.at[i], X.at[i], xs.at[0], xr.at[i], p, c).wait_recv()

        cols = slice(i * local_cols, (i + 1) * local_cols)
        xthi[cols, :], xtlo[cols, :] = split(X[i].T)

    D[...] = jnp.zeros_like(D)
    for h in range(H):
        rows = slice(h * hr, (h + 1) * hr)
        for i in range(q):
            u = c * q + i

            @pl.when(c > 0)
            def _():
                arrive(u, h)
                part[u, rows, :] += recv[u, rows, :]

            @pl.when(c < PC - 1)
            def _():
                arrive(PR + i, h)
                part[u, rows, :] += recv[PR + i, rows, :]

            cols = slice(i * local_cols, (i + 1) * local_cols)
            done = -part[u, rows, :]
            sel[rows, cols] = done
            D[:, cols] -= dot3(xthi[:, rows], xtlo[:, rows], *split(done))

    share = out.shape[1]

    def d_copy(t):
        pp = (p + t) % PR
        return remote(
            D.at[pl.ds(pl.multiple_of(pp * share, share), share)], E.at[t], ds_.at[t], dr.at[t], pp, c
        )

    for t in range(1, PR):
        d_copy(t).start()
    out[0] = diag[0] + D[pl.ds(pl.multiple_of(p * share, share), share), :]
    for t in range(1, PR):
        d_copy(t).wait_recv()
        out[0] += E[t]

    for t in range(1, PR):
        d_copy(t).wait_send()
    for t in range(1, Y):
        y_copy(t).wait_send()

    def drain_forward(yy, carry):
        forward(yy).wait_send()
        return carry

    lax.fori_loop(0, Y, drain_forward, 0)

    def drain(u, carry):
        @pl.when((c == pc) & (u // q != c))
        def _():
            x_copy(u).wait_send()

        @pl.when(u // q != c)
        def _():
            def one(h, inner):
                chain(u, h).wait_send()
                return inner

            lax.fori_loop(0, H, one, 0)

        return carry

    lax.fori_loop(0, PR, drain, 0)


def on_device(PR, PC, root_inverse, lower_blocks, block_pattern, diag_inverse):
    panel, depth = root_inverse.shape
    local_rows, local_cols = lower_blocks.shape
    H = panel // 128
    Y = PR // 2
    owned = local_cols * PR // PC
    q = owned // local_cols
    f32, bf16 = jnp.float32, jnp.bfloat16
    dma = pltpu.SemaphoreType.DMA
    vmem = pl.BlockSpec(memory_space=pltpu.VMEM)
    flops = 6 * panel * depth * local_cols * PR
    return pl.pallas_call(
        functools.partial(kernel, PR, PC, H),
        out_shape=(
            jax.ShapeDtypeStruct((panel, owned), f32),
            jax.ShapeDtypeStruct(diag_inverse.shape, f32),
        ),
        in_specs=[pl.BlockSpec(memory_space=pltpu.SMEM), vmem, vmem, vmem],
        out_specs=(vmem, vmem),
        scratch_shapes=[
            pltpu.VMEM((PR, local_rows, local_cols), f32),
            pltpu.VMEM((PR, panel, local_cols), f32),
            pltpu.VMEM((PR + q, panel, local_cols), f32),
            pltpu.VMEM((panel, depth), bf16),
            pltpu.VMEM((panel, depth), bf16),
            pltpu.VMEM((2, local_rows, local_cols), bf16),
            pltpu.VMEM((2, local_rows, local_cols), bf16),
            pltpu.VMEM((q, panel, local_cols), f32),
            pltpu.VMEM((owned, panel), bf16),
            pltpu.VMEM((owned, panel), bf16),
            pltpu.VMEM((owned, owned), f32),
            pltpu.VMEM((PR,) + diag_inverse.shape[1:], f32),
            dma((Y,)), dma((Y,)), dma((Y,)), dma((Y,)),
            dma((PR, H)), dma((PR + q, H)),
            dma((PR,)), dma((q,)), dma((PR,)), dma((PR,)),
        ],
        compiler_params=pltpu.CompilerParams(
            collective_id=0, has_side_effects=True, vmem_limit_bytes=56 * 1024 * 1024
        ),
        cost_estimate=pl.CostEstimate(flops=flops, bytes_accessed=8 * panel * depth, transcendentals=0),
    )(block_pattern, root_inverse, lower_blocks, diag_inverse)


def solution(mesh):
    placed = (
        P(("pole", "prow"), "pcol"),
        P(("pole", "pcol"), "prow"),
        P(),
        P(("pole", "pcol"), "prow", None),
    )
    return jax.shard_map(
        functools.partial(on_device, mesh.shape["prow"], mesh.shape["pcol"]),
        mesh=mesh,
        in_specs=placed,
        out_specs=(P(("pole", "prow"), "pcol"), P(("pole", "pcol"), "prow", None)),
        check_vma=False,
    )
```

time: 261 us -> 130 us (0.50)
  the two profiles are of different devices: /device:TPU:29 before, /device:TPU:1 now
where the time goes in v1:
time: 130 us; the launch traced here: 129 us
  Pallas kernels  124 us (95%)
  local copies, waits for them, and re-layouts  4.9 us (4%)
    pallas_call x1, Pallas kernels, on_device(): pl.pallas_call(functools.partial(kernel, PR, PC, H), out_shape=(jax.Shape...  124 us
    unnamed x3, local copies, waits for them, and re-layouts  4.9 us

profile of v1, /device:TPU:1, one launch (start us, length us, event | category | flops | bytes accessed | tf_op | source)
XLA Modules:
  0.0 129.3 jit_solution(7175454792780689179)
XLA Ops:
  0.6 1.4 %copy.6.pattern = s32[12,4]{1,0:T(8,128)} copy(s32[12,4]{0,1:T(4,128)} %param.6) | data formatting | bytes 384 | tf_op args[2]
  2.0 123.8 %shard_map.59 = (f32[768,256]{1,0:T(8,128)}, f32[1,64,256]{2,1,0:T(8,128)}) custom-call(s32[12,4]{1,0:T(8,128)} %copy.6.pattern, f32[768,768]{1,0:T(8,128)} %root.1, f32[768,256]{1,0:T(8,128)} %lower.1, f32[1,64,256]{2,1,0:T(8,128)} %diag.1), custom_call_target="tpu_custom_call" | custom-call | flops 3623878656 | bytes 4718592 | tf_op jit(solution)/shard_map/pallas_call | solution.py:230
  125.8 2.1 %copy.9 = f32[768,256]{1,0:T(8,128)} copy(f32[768,256]{1,0:T(8,128)} %get-tuple-element.4) | data formatting | bytes 1572864
  127.8 1.5 %copy.10 = f32[1,64,256]{2,1,0:T(8,128)} copy(f32[1,64,256]{2,1,0:T(8,128)} %get-tuple-element.5) | data formatting | bytes 131072

commit v2 on v1

--- a/solution.py
+++ b/solution.py
@@ -53,11 +53,22 @@
     for t in range(1, PC):
         pl.semaphore_signal(barrier, inc=1, device_id=(x, p, (c + t) % PC), device_id_type=MESH)
 
+    def away(r):
+        return (c * ratio + r != p) | (p // q != c)
+
+    for r in range(ratio):
+        @pl.when(away(r))
+        def _():
+            pl.semaphore_signal(
+                barrier, inc=1, device_id=(x, c * ratio + r, p // q), device_id_type=MESH
+            )
+
     supernode = p * local_cols // B
     for r in range(local_rows // B):
         keep = pattern[c * (local_rows // B) + r, supernode].astype(jnp.float32)
         G[p, r * B:(r + 1) * B, :] = lower[r * B:(r + 1) * B, :] * keep
-    pl.semaphore_wait(barrier, PR + PC - 2)
+    extra = sum(jnp.where(away(r), 1, 0) for r in range(ratio))
+    pl.semaphore_wait(barrier, PR + PC - 2 + extra)
 
     def y_copy(t):
         return remote(G.at[p], G.at[p], ygs.at[t], ygr.at[t], (y + t) % Y * 2 + core, c)
@@ -69,6 +80,17 @@
     for t in range(1, Y):
         y_copy(t).start()
     forward(y).start()
+
+    def x_copy(r):
+        return remote(
+            G.at[p, pl.ds(r * panel, panel)], X.at[p % q], xs.at[r], xr.at[p % q],
+            c * ratio + r, p // q,
+        )
+
+    for r in range(ratio):
+        @pl.when(away(r))
+        def _():
+            x_copy(r).start()
 
     def split_root(h, carry):
         rows = pl.ds(pl.multiple_of(h * hr, hr), hr)
@@ -92,11 +114,6 @@
             recv.at[slot, rows], recv.at[slot, rows], chs.at[0, h], chr_.at[slot, h], p, c
         ).wait_recv()
 
-    def x_copy(u):
-        return remote(
-            G.at[u, pl.ds(row_off, panel)], X.at[u % q], xs.at[u], xr.at[u % q], p, u // q
-        )
-
     def phase(t, carry):
         yy = (y + Y - t) % Y
 
@@ -109,10 +126,6 @@
         remote(G.at[other], G.at[other], fws.at[yy], fwr.at[yy], p, c).wait_recv()
         for i in range(2):
             u = yy * 2 + i
-
-            @pl.when((c == pc) & (u // q != c))
-            def _():
-                x_copy(u).start()
 
             lhi[i], llo[i] = split(G[u])
 
@@ -123,12 +136,7 @@
                 j = u // q
                 part[u, rows, :] = dot3(rhi[rows, :], rlo[rows, :], lhi[i], llo[i])
 
-                @pl.when(((j > c) & (c > 0)) | ((j < c) & (c < PC - 1)))
-                def _():
-                    arrive(u, h)
-                    part[u, rows, :] += recv[u, rows, :]
-
-                @pl.when(j != c)
+                @pl.when(((j > c) & (c == 0)) | ((j < c) & (c == PC - 1)))
                 def _():
                     chain(u, h).start()
 
@@ -139,12 +147,31 @@
 
     lax.fori_loop(0, Y, phase, 0)
 
+    def relay(h, carry):
+        rows = pl.ds(pl.multiple_of(h * hr, hr), hr)
+
+        def unit(u, inner):
+            j = u // q
+
+            @pl.when(((j > c) & (c > 0)) | ((j < c) & (c < PC - 1)))
+            def _():
+                arrive(u, h)
+                part[u, rows, :] += recv[u, rows, :]
+                chain(u, h).start()
+
+            return inner
+
+        lax.fori_loop(0, PR, unit, 0)
+        return carry
+
+    lax.fori_loop(0, H, relay, 0)
+
     for i in range(q):
-        @pl.when(c == pc)
+        @pl.when((c * q + i == p) & (c == pc))
         def _():
             X[i] = G[c * q + i, pl.ds(row_off, panel), :]
 
-        @pl.when(c != pc)
+        @pl.when((c * q + i != p) | (c != pc))
         def _():
             remote(X.at[i], X.at[i], xs.at[0], xr.at[i], p, c).wait_recv()
 
@@ -199,10 +226,6 @@
     lax.fori_loop(0, Y, drain_forward, 0)
 
     def drain(u, carry):
-        @pl.when((c == pc) & (u // q != c))
-        def _():
-            x_copy(u).wait_send()
-
         @pl.when(u // q != c)
         def _():
             def one(h, inner):
@@ -214,6 +237,10 @@
         return carry
 
     lax.fori_loop(0, PR, drain, 0)
+    for r in range(ratio):
+        @pl.when(away(r))
+        def _():
+            x_copy(r).wait_send()
 
 
 def on_device(PR, PC, root_inverse, lower_blocks, block_pattern, diag_inverse):

time: 130 us -> 125 us (0.962)
  the two profiles are of different devices: /device:TPU:1 before, /device:TPU:29 now
where the time goes in v2:
time: 125 us
  Pallas kernels  119 us (95%)
  local copies, waits for them, and re-layouts  4.9 us (4%)
    pallas_call x1, Pallas kernels, on_device(): pl.pallas_call(functools.partial(kernel, PR, PC, H), out_shape=(jax.Shape...  119 us
    unnamed x3, local copies, waits for them, and re-layouts  4.9 us

profile of v2, /device:TPU:29, one launch (start us, length us, event | category | flops | bytes accessed | tf_op | source)
XLA Modules:
  0.0 124.9 jit_solution(10815347815355622596)
XLA Ops:
  0.6 1.4 %copy.6.pattern = s32[12,4]{1,0:T(8,128)} copy(s32[12,4]{0,1:T(4,128)} %param.6) | data formatting | bytes 384 | tf_op args[2]
  2.0 119.4 %shard_map.59 = (f32[768,256]{1,0:T(8,128)}, f32[1,64,256]{2,1,0:T(8,128)}) custom-call(s32[12,4]{1,0:T(8,128)} %copy.6.pattern, f32[768,768]{1,0:T(8,128)} %root.1, f32[768,256]{1,0:T(8,128)} %lower.1, f32[1,64,256]{2,1,0:T(8,128)} %diag.1), custom_call_target="tpu_custom_call" | custom-call | flops 3623878656 | bytes 4718592 | tf_op jit(solution)/shard_map/pallas_call | solution.py:257
  121.4 2.1 %copy.9 = f32[768,256]{1,0:T(8,128)} copy(f32[768,256]{1,0:T(8,128)} %get-tuple-element.4) | data formatting | bytes 1572864
  123.5 1.5 %copy.10 = f32[1,64,256]{2,1,0:T(8,128)} copy(f32[1,64,256]{2,1,0:T(8,128)} %get-tuple-element.5) | data formatting | bytes 131072

commit v3 on v2

--- a/solution.py
+++ b/solution.py
@@ -87,11 +87,6 @@
             c * ratio + r, p // q,
         )
 
-    for r in range(ratio):
-        @pl.when(away(r))
-        def _():
-            x_copy(r).start()
-
     def split_root(h, carry):
         rows = pl.ds(pl.multiple_of(h * hr, hr), hr)
         rhi[rows, :], rlo[rows, :] = split(root[rows, :])
@@ -146,6 +141,11 @@
         return carry
 
     lax.fori_loop(0, Y, phase, 0)
+
+    for r in range(ratio):
+        @pl.when(away(r))
+        def _():
+            x_copy(r).start()
 
     def relay(h, carry):
         rows = pl.ds(pl.multiple_of(h * hr, hr), hr)

time: 125 us -> 142 us (1.14)
  Pallas kernels: 119 us -> 136 us
    pallas_call x1, Pallas kernels: 119 us -> 136 us  [on_device(): pl.pallas_call(functools.partial(kernel, PR, PC, H), out_shape=(jax.Shape...]
where the time goes in v3:
time: 142 us; the launch traced here: 141 us
  Pallas kernels  136 us (96%)
  local copies, waits for them, and re-layouts  4.9 us (3%)
    pallas_call x1, Pallas kernels, on_device(): pl.pallas_call(functools.partial(kernel, PR, PC, H), out_shape=(jax.Shape...  136 us
    unnamed x3, local copies, waits for them, and re-layouts  4.9 us

profile of v3, /device:TPU:29, one launch (start us, length us, event | category | flops | bytes accessed | tf_op | source)
XLA Modules:
  0.0 141.5 jit_solution(3598364924744653152)
XLA Ops:
  0.6 1.4 copy.6.pattern
  2.0 136.0 %shard_map.59 = (f32[768,256]{1,0:T(8,128)}, f32[1,64,256]{2,1,0:T(8,128)}) custom-call(s32[12,4]{1,0:T(8,128)} %copy.6.pattern, f32[768,768]{1,0:T(8,128)} %root.1, f32[768,256]{1,0:T(8,128)} %lower.1, f32[1,64,256]{2,1,0:T(8,128)} %diag.1), custom_call_target="tpu_custom_call" | custom-call | flops 3623878656 | bytes 4718592 | tf_op jit(solution)/shard_map/pallas_call | solution.py:257
  138.0 2.1 %copy.9 = f32[768,256]{1,0:T(8,128)} copy(f32[768,256]{1,0:T(8,128)} %get-tuple-element.4) | data formatting | bytes 1572864
  140.0 1.5 %copy.10 = f32[1,64,256]{2,1,0:T(8,128)} copy(f32[1,64,256]{2,1,0:T(8,128)} %get-tuple-element.5) | data formatting | bytes 131072
